TPU v7x, 32 devices: a whole 2x2x4 slice. The times are simulated.
32 devices in a mesh: lon: 4 (over y, x), lat: 8 (over z, core).
Axes of the slice: x: 2, y: 2, z: 4, core: 2. Of those that a mesh axis runs over, the one named last changes fastest.
Arguments:
- adjoint_in: float32 [5, 192, 192, 128], P(None, 'lon', 'lat'), may hold values from -6 to 6
- departures: float32 [4, 8, 1024, 128], P('lon', 'lat'), may hold values from -6 to 6
- obs_band: int32 [4, 8, 1024, 1], P('lon', 'lat'), may hold values from 0 to 7; in each aligned block of 1024 rows (0 to 1023, 1024 to 2047, ..., all dimensions but the last counted through in order) at most 384 rows name the same one
- obs_station: int32 [4, 8, 1024], P('lon', 'lat'), may hold values from 0 to 511
- obs_var: int32 [4, 8, 1024], P('lon', 'lat'), may hold values from 0 to 4
- counts: int32 [4, 8], P('lon', 'lat'), may hold values from 512 to 1024, as said below
- station_cell: int32 [4, 8, 512], P('lon', 'lat'), may hold values from 0 to 1151
- coefficients: float32 [3, 192, 192, 128], P(None, 'lon', 'lat'), as said below
Outputs:
- adjoint_out: float32 [5, 192, 192, 128], P(None, 'lon', 'lat')
Inputs may be any that keep to these rules, and one draw needn't show every extreme that they name: `obs_band`: among the 1024 blocks of one device at most 384 name the same band, and on some device exactly 384 do. `counts`: some device has exactly 1024 live blocks. `coefficients`: the diffusivity lies between 0.03 and 0.12.
All inputs are finite; a program needn't handle non-finite values.
Results may differ from a plain program's by a relative error of at most 0.00013.
Values sent between devices are 32-bit elements; how exact they have to be, the bound alone decides.
No kernel may reach another device: no remote copies, remote signals or barrier semaphores. Data moves between devices by JAX's collectives and lax.ppermute only.
A program may use at most 384 MiB of HBM per device.

v0:
```python
import functools

import jax
import jax.numpy as jnp
from jax import lax
from jax.experimental import pallas as pl
from jax.experimental.pallas import tpu as pltpu
from jax.sharding import PartitionSpec as P

ADVECT_SCALE = 0.2
LANES = 128
GROUP = 4
STRIDE = 1024
HEADER = 8
VMEM_LIMIT = 40 * 1024 * 1024
V = pltpu.VMEM


def in_vmem(array):
    return pltpu.with_memory_space_constraint(array, V)


def in_hbm(array):
    return pltpu.with_memory_space_constraint(array, pltpu.HBM)


def params():
    return pltpu.CompilerParams(vmem_limit_bytes=VMEM_LIMIT)


def start_all(copies):
    for copy in copies:
        copy.start()


def wait_all(copies):
    for copy in copies:
        copy.wait()


def run(copies):
    start_all(copies)
    wait_all(copies)


def pairs_of(axis, periodic):
    count = lax.axis_size(axis)
    near = [(i, i ^ 1) for i in range(count)]
    across = []
    for i in range(1, count, 2):
        if periodic or i + 1 < count:
            across += [(i, (i + 1) % count), ((i + 1) % count, i)]
    return near, across


def swap_sides(near, across, axis, periodic):
    near_pairs, across_pairs = pairs_of(axis, periodic)
    return lax.ppermute(near, axis, near_pairs), lax.ppermute(across, axis, across_pairs)


def near_side(low, high, axis="lat"):
    odd = (lax.axis_index(axis) & 1) == 1
    return jnp.where(odd, low, high), jnp.where(odd, high, low)


def pack_kernel(
    n, cap, stations, count_ref, band_ref, station_ref, var_ref, dep_ref, coef_ref, *rest
):
    half = n // 2
    own, swap = rest[:2]
    through = rest[2 : half + 1]
    near, across = rest[half + 1 : half + 3]
    (dep, band, station, var, edge, buf, pos_v, pos_s, sem) = rest[half + 3 :]
    me = lax.axis_index("lat")
    rows, lanes = band.shape
    lat_cells = coef_ref.shape[2]
    loads = [
        pltpu.make_async_copy(src, dst, sem.at[k])
        for k, (src, dst) in enumerate(
            (
                (band_ref, band),
                (station_ref, station),
                (var_ref, var),
                (dep_ref, dep),
                (coef_ref.at[:, :, pl.ds(0, 8)], edge.at[0]),
                (coef_ref.at[:, :, pl.ds(lat_cells - 8, 8)], edge.at[1]),
            )
        )
    ]
    start_all(loads)
    wait_all(loads[:3])
    count = count_ref[0, 0]
    slot = (
        lax.broadcasted_iota(jnp.int32, (rows, lanes), 0) * lanes
        + lax.broadcasted_iota(jnp.int32, (rows, lanes), 1)
    )
    far = (band[...] >> 1) - (me >> 1)
    far = jnp.where(far < 0, far + half, far)
    group = jnp.where((band[...] & 1) == (me & 1), far, far + half)
    group = jnp.where(slot < count, group, n)
    masks = jnp.concatenate([(group == s).astype(jnp.float32) for s in range(n)], axis=0)
    before = lax.broadcasted_iota(jnp.int32, (lanes, lanes), 0) < lax.broadcasted_iota(
        jnp.int32, (lanes, lanes), 1
    )
    prefix = jnp.dot(masks, before.astype(jnp.float32), preferred_element_type=jnp.float32)
    totals = jnp.dot(
        masks, jnp.ones((lanes, lanes), jnp.float32), preferred_element_type=jnp.float32
    )
    a = lax.broadcasted_iota(jnp.int32, (rows * n, rows * n), 0)
    b = lax.broadcasted_iota(jnp.int32, (rows * n, rows * n), 1)
    earlier = ((a // rows == b // rows) & (b < a)).astype(jnp.float32)
    offset = jnp.dot(earlier, totals, preferred_element_type=jnp.float32)
    ranks = (prefix + offset).astype(jnp.int32)
    rank = jnp.zeros((rows, lanes), jnp.int32)
    for s in range(n):
        rank = jnp.where(group == s, ranks[s * rows : (s + 1) * rows], rank)
    pos_v[...] = group * STRIDE + rank
    place_map = pltpu.make_async_copy(pos_v, pos_s, sem.at[0])
    place_map.start()
    code = var[...] * stations + station[...]
    upper = (code >> 6).astype(jnp.float32)
    lower = (code & 63).astype(jnp.float32)
    width = -(-cap // lanes) * lanes
    which = lax.broadcasted_iota(jnp.int32, (n, lanes), 0)
    order = lax.broadcasted_iota(jnp.int32, (width, lanes), 0)
    codes = jnp.zeros((2 * n, width), jnp.float32)
    for k in range(rows):
        mine = which == group[k : k + 1]
        parts = jnp.concatenate(
            [jnp.where(mine, upper[k : k + 1], 0.0), jnp.where(mine, lower[k : k + 1], 0.0)], 0
        )
        codes += lax.dot_general(
            parts,
            (order == rank[k : k + 1]).astype(jnp.float32),
            (((1,), (1,)), ((), ())),
            preferred_element_type=jnp.float32,
        )
    codes = codes[:n] * 64.0 + codes[n:]
    counts = offset + totals
    size = cap + HEADER

    def target(s):
        if s == 0:
            return own, 0
        if s < half:
            return through[s - 1], 0
        return swap, (s - half) * size

    for s in range(n):
        to, at = target(s)
        for j in range(width // lanes):
            to[pl.ds(at + cap + j, 1), :] = codes[s : s + 1, j * lanes : (j + 1) * lanes]
        to[pl.ds(at + cap + HEADER - 1, 1), :] = counts[(s + 1) * rows - 1 : (s + 1) * rows]
    wait_all(loads[3:])
    fields, lons = edge.shape[1:3]
    odd = me & 1

    def strip(i, carry):
        for f in range(fields):
            near[pl.ds((f * lons + i) * 2, 2), :] = edge[1 - odd, f, i, pl.ds(6 - 6 * odd, 2), :]
            across[pl.ds((f * lons + i) * 2, 2), :] = edge[odd, f, i, pl.ds(6 * odd, 2), :]
        return carry

    lax.fori_loop(0, lons, strip, 0)
    place_map.wait()

    def place(g, carry):
        base = pl.multiple_of(g * 16, 16)
        row, col = base >> 7, base & 127
        for k in range(16):
            buf[pl.ds(pos_s[row, col + k], 1), :] = dep[pl.ds(base + k, 1), :]
        return carry

    lax.fori_loop(0, (count + 15) >> 4, place, 0)
    for s in range(n):
        to, at = target(s)
        to[pl.ds(at, cap), :] = buf[pl.ds(s * STRIDE, cap), :]


def pack(n, cap, stations, count, band, station, var, dep, coef):
    rows = dep.shape[0] // LANES
    fields, lons = coef.shape[:2]
    size, half = cap + HEADER, n // 2
    strip = (fields * lons * 2, LANES)
    shapes = [(size, LANES), (half * size, LANES)]
    shapes += [
        (size if s == half // 2 else 2 * size, LANES) for s in range(1, half)
    ] + [strip, strip]
    hbm = pl.BlockSpec(memory_space=pltpu.HBM)
    vm = pl.BlockSpec(memory_space=V)
    return pl.pallas_call(
        functools.partial(pack_kernel, n, cap, stations),
        out_shape=tuple(V(shape, jnp.float32) for shape in shapes),
        in_specs=[pl.BlockSpec(memory_space=pltpu.SMEM)] + [hbm] * 5,
        out_specs=(vm,) * len(shapes),
        scratch_shapes=[
            V(dep.shape, jnp.float32),
            V((rows, LANES), jnp.int32),
            V((rows, LANES), jnp.int32),
            V((rows, LANES), jnp.int32),
            V((2, fields, lons, 8, LANES), jnp.float32),
            V((n * STRIDE + HEADER + STRIDE, LANES), jnp.float32),
            V((rows, LANES), jnp.int32),
            pltpu.SMEM((rows, LANES), jnp.int32),
            pltpu.SemaphoreType.DMA((6,)),
        ],
        compiler_params=params(),
        name="pack",
    )(count, *(in_hbm(array) for array in (band, station, var, dep, coef)))


def relay_kernel(shifts, size, swapped, *rest):
    for s, to in zip(shifts, rest[len(rest) - len(shifts) :]):
        to[pl.ds(size, size), :] = swapped[pl.ds(s * size, size), :]


def relay(swapped, through, shifts, size, after=()):
    k = len(shifts)
    vm = pl.BlockSpec(memory_space=V)
    picked = [through[s - 1] for s in shifts]
    return pl.pallas_call(
        functools.partial(relay_kernel, shifts, size),
        out_shape=tuple(V(array.shape, jnp.float32) for array in picked),
        in_specs=[vm] * (k + 1 + len(after)),
        out_specs=(vm,) * k,
        input_output_aliases={j + 1: j for j in range(k)},
        compiler_params=params(),
        name="relay",
    )(in_vmem(swapped), *(in_vmem(array) for array in (*picked, *after)))


def alone_kernel(start, swapped, *rest):
    to = rest[-1]
    to[...] = swapped[pl.ds(start, to.shape[0]), :]


def alone(swapped, s, size, after=()):
    vm = pl.BlockSpec(memory_space=V)
    return pl.pallas_call(
        functools.partial(alone_kernel, s * size),
        out_shape=V((size, LANES), jnp.float32),
        in_specs=[vm] * (1 + len(after)),
        out_specs=vm,
        compiler_params=params(),
        name="alone",
    )(in_vmem(swapped), *(in_vmem(array) for array in after))


def open_header(packet, base, cap, view, header, sem):
    view[...] = packet[pl.ds(base + cap, HEADER), :].astype(jnp.int32)
    copy = pltpu.make_async_copy(view, header, sem)
    copy.start()
    return copy


def scatter_packet(table_ref, packet, start, header, state):
    unroll = 8
    count = header[HEADER - 1, 0]

    def some(g, carry):
        base = g * unroll
        major, minor = base >> 7, base & 127
        rows = [table_ref[0, header[major, minor + k]] for k in range(unroll)]
        for k in range(unroll):
            state[pl.ds(rows[k], 1), :] += packet[pl.ds(start + base + k, 1), :]
        return carry

    def one(j, carry):
        row = table_ref[0, header[j >> 7, j & 127]]
        state[pl.ds(row, 1), :] += packet[pl.ds(start + j, 1), :]
        return carry

    whole = count >> 3
    lax.fori_loop(0, whole, some, 0)
    lax.fori_loop(whole * unroll, count, one, 0)


def first_kernel(
    k, lons, lats, cap, table_ref, adjoint_ref, *rest
):
    packets, (state, full) = rest[:k], rest[len(rest) - 2 * k - 3 : len(rest) - 2 * k - 1]
    rest = rest[len(rest) - 2 * k - 1 :]
    views, headers, sem = rest[:k], rest[k : 2 * k], rest[2 * k]
    span = lats + 4
    ring = (lons + 4) * span
    nv = state.shape[0] // ring
    load = pltpu.make_async_copy(adjoint_ref, full, sem.at[0])
    load.start()
    opened = [
        open_header(packets[j], 0, cap, views[j], headers[j], sem.at[j + 1]) for j in range(k)
    ]
    load.wait()

    def fill(i, carry):
        for v in range(nv):
            to = v * ring + (i + 2) * span + 2
            at = (v * lons + i) * lats
            for r in range(0, lats, 8):
                state[pl.ds(to + r, 8), :] = full[pl.ds(pl.multiple_of(at + r, 8), 8), :]
        return carry

    lax.fori_loop(0, lons, fill, 0)
    wait_all(opened)
    for j in range(k):
        scatter_packet(table_ref, packets[j], 0, headers[j], state)


def scatter_first(table, adjoint, packets, cap, shape, after=()):
    nv, lons, lats = shape
    k = len(packets)
    hbm = pl.BlockSpec(memory_space=pltpu.HBM)
    ring = (lons + 4) * (lats + 4)
    return pl.pallas_call(
        functools.partial(first_kernel, k, lons, lats, cap),
        out_shape=V((nv * ring, LANES), jnp.float32),
        in_specs=[pl.BlockSpec(memory_space=pltpu.SMEM), hbm]
        + [pl.BlockSpec(memory_space=V)] * (k + len(after)),
        out_specs=pl.BlockSpec(memory_space=V),
        scratch_shapes=[
            V(adjoint.shape, jnp.float32),
            *[V((HEADER, LANES), jnp.int32)] * k,
            *[pltpu.SMEM((HEADER, LANES), jnp.int32)] * k,
            pltpu.SemaphoreType.DMA((k + 1,)),
        ],
        compiler_params=params(),
        name="scatter_own",
    )(table, in_hbm(adjoint), *(in_vmem(array) for array in (*packets, *after)))


def more_kernel(k, lons, lats, cap, last, table_ref, *rest):
    size = cap + HEADER
    packets = [(rest[j], base) for j in range(k) for base in range(0, rest[j].shape[0], size)]
    m = len(packets)
    rest = rest[len(rest) - (3 if last else 1) - 2 * m - 1 :]
    outs, rest = rest[: 3 if last else 1], rest[3 if last else 1 :]
    views, headers, sem = rest[:m], rest[m : 2 * m], rest[2 * m]
    state = outs[0]
    opened = [
        open_header(*packets[j], cap, views[j], headers[j], sem.at[j]) for j in range(m)
    ]
    wait_all(opened)
    for j in range(m):
        scatter_packet(table_ref, *packets[j], headers[j], state)
    if not last:
        return
    near, across = outs[1:]
    span = lats + 4
    ring = (lons + 4) * span
    nv = state.shape[0] // ring
    near_row, across_row = near_side(2, lats)

    def strip(i, carry):
        for v in range(nv):
            at = v * ring + (i + 2) * span
            to = (v * lons + i) * 2
            near[pl.ds(to, 2), :] = state[pl.ds(at + near_row, 2), :]
            across[pl.ds(to, 2), :] = state[pl.ds(at + across_row, 2), :]
        return carry

    lax.fori_loop(0, lons, strip, 0)


def scatter_more(table, state, packets, cap, shape, last, after=()):
    nv, lons, lats = shape
    k = len(packets)
    m = sum(packet.shape[0] // (cap + HEADER) for packet in packets)
    vm = pl.BlockSpec(memory_space=V)
    out = V(state.shape, jnp.float32)
    strip = V((nv * lons * 2, LANES), jnp.float32)
    return pl.pallas_call(
        functools.partial(more_kernel, k, lons, lats, cap, last),
        out_shape=(out, strip, strip) if last else out,
        in_specs=[pl.BlockSpec(memory_space=pltpu.SMEM)] + [vm] * (k + 1 + len(after)),
        out_specs=(vm, vm, vm) if last else vm,
        input_output_aliases={k + 1: 0},
        scratch_shapes=[V((HEADER, LANES), jnp.int32)] * m
        + [pltpu.SMEM((HEADER, LANES), jnp.int32)] * m
        + [pltpu.SemaphoreType.DMA((m,))],
        compiler_params=params(),
        name="scatter_last" if last else "scatter_more",
    )(
        table,
        *(in_vmem(packet) for packet in packets),
        in_vmem(state),
        *(in_vmem(array) for array in after),
    )


def widen_kernel(coef_ref, near_ref, across_ref, after, ring_out, near_lon, across_lon, own, sem):
    fields, lons, lats, _ = coef_ref.shape
    span = lats + 4
    ring = (lons + 4) * span
    near_row, across_row = near_side(0, lats + 2)
    near_at, across_at = near_side(2 * span, lons * span, "lon")
    run([pltpu.make_async_copy(coef_ref, own, sem)])

    def fill(i, carry):
        for f in range(fields):
            to = f * ring + (i + 2) * span
            at = (f * lons + i) * 2
            for r in range(0, lats, 8):
                ring_out[pl.ds(to + 2 + r, 8), :] = own[f, i, r : r + 8]
            ring_out[pl.ds(to + near_row, 2), :] = near_ref[pl.ds(at, 2), :]
            ring_out[pl.ds(to + across_row, 2), :] = across_ref[pl.ds(at, 2), :]
        return carry

    lax.fori_loop(0, lons, fill, 0)
    take_lons(ring_out, near_lon, across_lon, fields, ring, 2 * span, near_at, across_at)


def take_lons(ring_ref, near, across, count, ring, size, near_at, across_at):
    for f in range(count):
        near[pl.ds(f * size, size), :] = ring_ref[pl.ds(f * ring + near_at, size), :]
        across[pl.ds(f * size, size), :] = ring_ref[pl.ds(f * ring + across_at, size), :]


def put_lons(ring_ref, near, across, count, ring, size, near_at, across_at):
    for f in range(count):
        ring_ref[pl.ds(f * ring + near_at, size), :] = near[pl.ds(f * size, size), :]
        ring_ref[pl.ds(f * ring + across_at, size), :] = across[pl.ds(f * size, size), :]


def widen(coef, near, across, after):
    fields, lons, lats, _ = coef.shape
    span = lats + 4
    vm = pl.BlockSpec(memory_space=V)
    edge = V((fields * 2 * span, LANES), jnp.float32)
    return pl.pallas_call(
        widen_kernel,
        out_shape=(V((fields * (lons + 4) * span, LANES), jnp.float32), edge, edge),
        in_specs=[pl.BlockSpec(memory_space=pltpu.HBM), vm, vm, vm],
        out_specs=(vm, vm, vm),
        scratch_shapes=[V(coef.shape, jnp.float32), pltpu.SemaphoreType.DMA],
        compiler_params=params(),
        name="widen",
    )(in_hbm(coef), in_vmem(near), in_vmem(across), in_vmem(after))


def combine_kernel(lons, lats, ring_ref, near, across, out_ref, field):
    me = lax.axis_index("lat")
    total = lats * lax.axis_size("lat")
    span, rim = lats + 4, lats + 2
    ring = (lons + 4) * span
    size = rim_rows(lons, lats)
    field[...] = ring_ref[...]
    ends = near_side(0, (lons + 2) * span, "lon")
    put_lons(field, near, across, field.shape[0] // ring, ring, 2 * span, *ends)
    lev = lax.broadcasted_iota(jnp.int32, (8, LANES), 1)
    row = lax.broadcasted_iota(jnp.int32, (8, LANES), 0)

    def one(i, carry):
        for r in chunks(rim):
            lat = row + (r - 1) + me * lats
            inside = (lat >= 0) & (lat < total)
            at = (i + 1) * span + r + 1

            def wind(f, shift, at=at):
                return ADVECT_SCALE * field[pl.ds(f * ring + at + shift, 8), :]

            def half(shift, at=at):
                return 0.5 * field[pl.ds(2 * ring + at + shift, 8), :]

            mine = half(0)
            east_factor = wind(0, 0) + (mine + half(span))
            west_factor = (mine + half(-span)) - wind(0, -span)
            north_factor = wind(1, 0) + (mine + half(1))
            south_factor = (mine + half(-1)) - wind(1, -1)
            up = jnp.where(lev < LANES - 1, mine + pltpu.roll(mine, LANES - 1, 1), 0.0)
            down = jnp.where(lev > 0, mine + pltpu.roll(mine, 1, 1), 0.0)
            centre = 1.0 - (
                ((east_factor + west_factor) + (north_factor + south_factor)) + (up + down)
            )
            factors = (centre, east_factor, west_factor, north_factor, south_factor, up, down)
            for k, value in enumerate(factors):
                out_ref[pl.ds(k * size + i * rim + r, 8), :] = jnp.where(inside, value, 0.0)
        return carry

    lax.fori_loop(0, lons + 2, one, 0)


def combine(ring, near, across, lons, lats):
    vm = pl.BlockSpec(memory_space=V)
    return pl.pallas_call(
        functools.partial(combine_kernel, lons, lats),
        out_shape=V((7 * rim_rows(lons, lats), LANES), jnp.float32),
        in_specs=[vm, vm, vm],
        out_specs=vm,
        scratch_shapes=[V(ring.shape, jnp.float32)],
        compiler_params=params(),
        name="combine",
    )(in_vmem(ring), in_vmem(near), in_vmem(across))


def rim_rows(lons, lats):
    return -(-(lons + 2) * (lats + 2) // 8) * 8


def chunks(rows):
    starts = list(range(0, rows - 7, 8))
    if starts[-1] + 8 < rows:
        starts.append(rows - 8)
    return starts


def shift_matrix():
    k = lax.broadcasted_iota(jnp.int32, (2 * LANES, 2 * LANES), 0) & (LANES - 1)
    j = lax.broadcasted_iota(jnp.int32, (2 * LANES, 2 * LANES), 1)
    take = ((j < LANES) & (k == j + 1)) | ((j >= LANES) & (k == j - LANES - 1))
    return take.astype(jnp.float32).astype(jnp.bfloat16)


def shifted(centres, matrix):
    block = jnp.concatenate(centres, axis=0)
    high = block.astype(jnp.bfloat16)
    low = (block - high.astype(jnp.float32)).astype(jnp.bfloat16)
    both = jnp.dot(
        jnp.concatenate([high, low], axis=1), matrix, preferred_element_type=jnp.float32
    )
    return [
        (both[8 * k : 8 * k + 8, :LANES], both[8 * k : 8 * k + 8, LANES:])
        for k in range(len(centres))
    ]


def rolled(centre):
    return pltpu.roll(centre, LANES - 1, 1), pltpu.roll(centre, 1, 1)


def weighted(factors, source, at, east, rows=None, levels=None):
    rows = rows or (lambda start: pl.ds(start, 8))
    centre = source[rows(at), :]
    above, below = levels or rolled(centre)
    total = factors[0] * centre + factors[1] * source[rows(at + east), :]
    other = factors[2] * source[rows(at - east), :] + factors[3] * source[rows(at + 1), :]
    third = factors[4] * source[rows(at - 1), :] + factors[5] * above
    return (total + other) + (third + factors[6] * below)


def step_rows(coef_ref, source, nv, spots, stride, east, put, matrix):
    size = coef_ref.shape[0] // 7
    levels = [None] * (len(spots) * nv)
    if matrix is not None:
        part = int(len(levels) * 0.5) // 2 * 2
        levels[:part] = shifted(
            [source[pl.ds(v * stride + at, 8), :] for _, at in spots for v in range(nv)][:part],
            matrix,
        )
    for k, (row, at) in enumerate(spots):
        factors = [coef_ref[pl.ds(f * size + row, 8), :] for f in range(7)]
        for v in range(nv):
            put(
                k,
                v,
                weighted(
                    factors, source, v * stride + at, east, levels=levels[k * nv + v]
                ),
            )


def first_step(coef_ref, state, mid, nv, lons, lats, places, starts, matrix=None):
    span, rim = lats + 4, lats + 2
    ring, size = (lons + 4) * span, rim_rows(lons, lats)
    spots = [(i * rim + r, (i + 1) * span + r + 1) for i in places for r in starts]

    def put(k, v, value):
        mid[pl.ds(v * size + spots[k][0], 8), :] = value

    step_rows(coef_ref, state, nv, spots, ring, span, put, matrix)


def first_step_along(coef_ref, state, mid, nv, lons, lats, i, r):
    span, rim = lats + 4, lats + 2
    ring, size = (lons + 4) * span, rim_rows(lons, lats)

    def rim_at(start):
        return pl.ds(start, 8, stride=rim)

    def ring_at(start):
        return pl.ds(start, 8, stride=span)

    factors = [coef_ref[rim_at(k * size + i * rim + r), :] for k in range(7)]
    for v in range(nv):
        mid[rim_at(v * size + i * rim + r), :] = weighted(
            factors, state, v * ring + (i + 1) * span + r + 1, span, ring_at
        )


def second_step(coef_ref, mid, out, nv, lons, lats, places, place, matrix=None):
    rim = lats + 2
    spots = [
        ((i + 1) * rim + r + 1, (i + 1) * rim + r + 1) for i in places for r in range(0, lats, 8)
    ]
    each = lats // 8

    def put(k, v, value):
        at = place(v, k // each) + (k % each) * 8
        out[pl.ds(pl.multiple_of(at, 8), 8), :] = value

    step_rows(coef_ref, mid, nv, spots, rim_rows(lons, lats), rim, put, matrix)


def insert_kernel(lons, lats, state_in, near, across, state, near_lon, across_lon):
    span = lats + 4
    ring = (lons + 4) * span
    nv = state.shape[0] // ring

    near_row, across_row = near_side(0, lats + 2)

    def strip(i, carry):
        for v in range(nv):
            at = v * ring + (i + 2) * span
            frm = (v * lons + i) * 2
            state[pl.ds(at + near_row, 2), :] = near[pl.ds(frm, 2), :]
            state[pl.ds(at + across_row, 2), :] = across[pl.ds(frm, 2), :]
        return carry

    lax.fori_loop(0, lons, strip, 0)
    ends = near_side(2 * span, lons * span, "lon")
    take_lons(state, near_lon, across_lon, nv, ring, 2 * span, *ends)


def insert(state, near, across, shape):
    nv, lons, lats = shape
    vm = pl.BlockSpec(memory_space=V)
    edge = V((nv * 2 * (lats + 4), LANES), jnp.float32)
    return pl.pallas_call(
        functools.partial(insert_kernel, lons, lats),
        out_shape=(V(state.shape, jnp.float32), edge, edge),
        in_specs=[vm] * 3,
        out_specs=(vm,) * 3,
        input_output_aliases={0: 0},
        compiler_params=params(),
        name="insert",
    )(in_vmem(state), in_vmem(near), in_vmem(across))


def early_kernel(nv, lons, lats, coef_ref, state, mid):
    starts = [r + 2 for r in chunks(lats - 2)]
    matrix = shift_matrix()

    def first(i, carry):
        at = jnp.minimum(2 + GROUP * i, lons - GROUP)
        places = [at + k for k in range(GROUP)]
        first_step(coef_ref, state, mid, nv, lons, lats, places, starts, matrix)
        return carry

    lax.fori_loop(0, -(-(lons - 2) // GROUP), first, 0)


def early(coef, state, shape):
    nv, lons, lats = shape
    vm = pl.BlockSpec(memory_space=V)
    return pl.pallas_call(
        functools.partial(early_kernel, nv, lons, lats),
        out_shape=V((nv * rim_rows(lons, lats), LANES), jnp.float32),
        in_specs=[vm, vm],
        out_specs=vm,
        compiler_params=params(),
        name="early",
    )(in_vmem(coef), in_vmem(state))


def inner_kernel(lons, lats, coef_ref, state, mid_in, mid, out_ref, out, sem):
    nv = out.shape[0] // (lons * lats)
    cells = lons * lats
    for r in (0, 1, lats, lats + 1):

        def first(k, carry, r=r):
            i = jnp.minimum(2 + 8 * k, lons - 8)
            first_step_along(coef_ref, state, mid, nv, lons, lats, i, r)
            return carry

        lax.fori_loop(0, -(-(lons - 2) // 8), first, 0)

    matrix = shift_matrix()

    def second(i, carry):
        second_step(
            coef_ref,
            mid,
            out,
            nv,
            lons,
            lats,
            [2 + GROUP * i + k for k in range(GROUP)],
            lambda v, k: v * cells + (2 + GROUP * i + k) * lats,
            matrix,
        )
        return carry

    parts = 4
    groups = (lons - 4) // GROUP
    ends = [0] + [groups * p // parts for p in range(1, parts)] + [groups]
    edges = [2 + GROUP * g for g in ends]
    copies = []
    for p in range(parts):
        lax.fori_loop(ends[p], ends[p + 1], second, 0)
        for v in range(nv):
            span = pl.ds(v * cells + edges[p] * lats, (edges[p + 1] - edges[p]) * lats)
            copy = pltpu.make_async_copy(out.at[span], out_ref.at[span], sem.at[p * nv + v])
            copy.start()
            copies.append(copy)
    wait_all(copies)


def inner(coef, state, mid, shape):
    nv, lons, lats = shape
    vm = pl.BlockSpec(memory_space=V)
    return pl.pallas_call(
        functools.partial(inner_kernel, lons, lats),
        out_shape=(
            V(mid.shape, jnp.float32),
            jax.ShapeDtypeStruct((nv * lons * lats, LANES), jnp.float32),
        ),
        in_specs=[vm, vm, vm],
        out_specs=(vm, pl.BlockSpec(memory_space=pltpu.HBM)),
        input_output_aliases={2: 0},
        scratch_shapes=[
            V((nv * lons * lats, LANES), jnp.float32),
            pltpu.SemaphoreType.DMA((4 * nv,)),
        ],
        compiler_params=params(),
        name="inner",
    )(in_vmem(coef), in_vmem(state), in_vmem(mid))


def outer_kernel(
    lons, lats, coef_ref, state_in, mid_in, near, across, out_in, state, mid, out_ref, out, sem
):
    span = lats + 4
    ring = (lons + 4) * span
    nv = state.shape[0] // ring
    cells = lons * lats
    ends = near_side(0, (lons + 2) * span, "lon")
    put_lons(state, near, across, nv, ring, 2 * span, *ends)

    def first(k, carry):
        i = jnp.where(k < 2, k, lons - 2 + k)
        first_step(coef_ref, state, mid, nv, lons, lats, (i,), chunks(lats + 2))
        return carry

    lax.fori_loop(0, 4, first, 0)

    def second(k, carry):
        i = jnp.where(k < 2, k, lons - 4 + k)
        second_step(
            coef_ref, mid, out, nv, lons, lats, (i,), lambda v, _: (v * 4 + k) * lats
        )
        return carry

    lax.fori_loop(0, 4, second, 0)
    copies = []
    for v in range(nv):
        for side, at in ((0, 0), (1, lons - 2)):
            copies.append(
                pltpu.make_async_copy(
                    out.at[pl.ds((v * 4 + 2 * side) * lats, 2 * lats)],
                    out_ref.at[pl.ds(v * cells + at * lats, 2 * lats)],
                    sem.at[v * 2 + side],
                )
            )
    run(copies)


def outer(coef, state, mid, near, across, out, shape):
    nv, lons, lats = shape
    vm = pl.BlockSpec(memory_space=V)
    hbm = pl.BlockSpec(memory_space=pltpu.HBM)
    return pl.pallas_call(
        functools.partial(outer_kernel, lons, lats),
        out_shape=(
            V(state.shape, jnp.float32),
            V(mid.shape, jnp.float32),
            jax.ShapeDtypeStruct(out.shape, jnp.float32),
        ),
        in_specs=[vm] * 5 + [hbm],
        out_specs=(vm, vm, hbm),
        input_output_aliases={1: 0, 2: 1, 5: 2},
        scratch_shapes=[V((nv * 4 * lats, LANES), jnp.float32), pltpu.SemaphoreType.DMA((2 * nv,))],
        compiler_params=params(),
        name="outer",
    )(in_vmem(coef), in_vmem(state), in_vmem(mid), in_vmem(near), in_vmem(across), out)[2]


def body(
    adjoint_in, departures, obs_band, obs_station, obs_var, counts, station_cell, coefficients
):
    nv, lons, lats, levels = adjoint_in.shape
    shape = (nv, lons, lats)
    slots = departures.shape[2]
    n = lax.axis_size("lat")
    cap = -(-3 * slots // n // 8) * 8
    stations = station_cell.shape[2]
    square = (slots // LANES, LANES)
    own, swap, *rest = pack(
        n,
        cap,
        stations,
        counts,
        obs_band.reshape(square),
        obs_station.reshape(square),
        obs_var.reshape(square),
        departures.reshape(slots, levels),
        coefficients,
    )
    through, (near, across) = rest[:-2], rest[-2:]
    swapped = lax.ppermute(swap, "lat", [(i, i ^ 1) for i in range(n)])
    near, across = swap_sides(near, across, "lat", False)
    size = cap + HEADER
    order = sorted(range(1, n // 2), key=lambda s: abs(4 * s - n))
    cell = station_cell.reshape(1, stations)
    span = lats + 4
    spot = (cell // lats + 2) * span + cell % lats + 2
    tile = (lons + 4) * span
    table = jnp.concatenate([spot + v * tile for v in range(nv)], axis=1)
    def send(s, packet):
        return lax.ppermute(packet, "lat", [(i, (i + 2 * s) % n) for i in range(n)])

    def send_pairs(shifts, after):
        return [
            send(s, packet)
            for s, packet in zip(shifts, relay(swapped, through, shifts, size, after))
        ]

    middle = 1 + (len(order) - 1) // 2
    adjoint = adjoint_in.reshape(nv * lons * lats, levels)
    ahead = send(order[0], through[order[0] - 1])
    second = send_pairs(order[1:middle], ())
    ring, near, across = widen(coefficients, near, across, swapped)
    third = send_pairs(order[middle:], (ring,))
    near, across = swap_sides(near, across, "lon", True)
    coef = combine(ring, near, across, lons, lats)
    state = scatter_first(table, adjoint, [own, swapped, ahead], cap, shape, (coef,))
    moved = [send(order[0], alone(swapped, order[0], size, (state,)))]
    state = scatter_more(table, state, second, cap, shape, False)
    state = scatter_more(table, state, third, cap, shape, False)
    state, near, across = scatter_more(table, state, moved, cap, shape, True)
    near, across = swap_sides(near, across, "lat", False)
    mid = early(coef, state, shape)
    state, near, across = insert(state, near, across, shape)
    near, across = swap_sides(near, across, "lon", True)
    mid, out = inner(coef, state, mid, shape)
    out = outer(coef, state, mid, near, across, out, shape)
    return out.reshape(adjoint_in.shape)


def solution(mesh):
    in_specs = (
        P(None, "lon", "lat", None),
        P("lon", "lat", None, None),
        P("lon", "lat", None, None),
        P("lon", "lat", None),
        P("lon", "lat", None),
        P("lon", "lat"),
        P("lon", "lat", None),
        P(None, "lon", "lat", None),
    )
    out_specs = P(None, "lon", "lat", None)
    return jax.shard_map(body, mesh=mesh, in_specs=in_specs, out_specs=out_specs, check_vma=False)
```

profile of v0, /device:TPU:1, one launch (start us, length us, event | category | flops | bytes accessed | tf_op | source)
XLA Modules:
  0.0 71.1 jit_solution(10904132334305883943)
XLA Ops:
  0.7 4.5 %pack.1 = (f32[392,128]{1,0:T(8,128)S(1)}, f32[1568,128]{1,0:T(8,128)S(1)}, f32[784,128]{1,0:T(8,128)S(1)}, f32[392,128]{1,0:T(8,128)S(1)}, f32[784,128]{1,0:T(8...) custom-call(s32[1,1]{1,0:T(1,128)S(6)} %copy.33.count_ref, s32[8,128]{1,0:T(8,128)} %bitcast.26, ...), custom_call_target="tpu_custom_call" | custom-call | tf_op jit(solution)/shard_map/pack/pallas_call | solution.py:191
  5.1 0.1 collective-permute-start
  5.2 4.2 %collective-permute-start.1 = (f32[288,128]{1,0:T(8,128)S(1)}, f32[288,128]{1,0:T(8,128)S(1)}, u32[]{:S(2)}, u32[]{:S(2)}) collective-permute-start(f32[288,128]{1,0:T(8,128)S(1)} %get-tuple-element.25), channel_id=1, source_target_pairs={{1,2},{2,1},{3,4},{4,3},{5,6},{6,5},{9,10},{10,9},{11,12},{12,11},... | collective-permute-start | bytes 442376 | tf_op jit(solution)/shard_map/ppermute | solution.py:58
  9.5 2.4 %collective-permute-start.5 = (f32[392,128]{1,0:T(8,128)S(1)}, f32[392,128]{1,0:T(8,128)S(1)}, u32[]{:S(2)}, u32[]{:S(2)}) collective-permute-start(f32[392,128]{1,0:T(8,128)S(1)} %get-tuple-element.31), channel_id=1, source_target_pairs={{0,4},{1,5},{2,6},{3,7},{4,0},{5,1},{6,2},{7,3},{8,12},{9,13},{10,... | collective-permute-start | bytes 602120 | tf_op jit(solution)/shard_map/ppermute | solution.py:817
  11.8 0.0 collective-permute-start.2
  11.8 0.7 constant_dynamic-update-slice_fusion.4
  12.6 1.6 %collective-permute-done.2.after.rest_1_.swapped = f32[1568,128]{1,0:T(8,128)S(1)} collective-permute-done((f32[1568,128]{1,0:T(8,128)S(1)}, f32[1568,128]{1,0:T(8,128)S(1)}, u32[]{:S(2)}, u32[]{:S(2)}) %collective-permute-start.2) | collective-permute-done | bytes 802848 | tf_op jit(solution)/shard_map/ppermute | solution.py:807
  14.2 0.5 collective-permute-start.8
  14.7 0.0 collective-permute-done.1.across_ref
  14.7 1.9 %widen.1 = (f32[4368,128]{1,0:T(8,128)S(1)}, f32[168,128]{1,0:T(8,128)S(1)}, f32[168,128]{1,0:T(8,128)S(1)}) custom-call(f32[3,48,24,128]{3,2,1,0:T(8,128)} %coef_ref.3, f32[288,128]{1,0:T(8,128)S(1)} %collective-permute-done.near_ref, f32[288,128]{1,0:T(8,128)S(1)} %collective-permute-done.1.across_ref, ...), custom_call_target="tpu_custom_call" | custom-call | tf_op jit(solution)/shard_map/widen/pallas_call | solution.py:428
  16.6 1.0 %collective-permute-start.3 = (f32[168,128]{1,0:T(8,128)S(1)}, f32[168,128]{1,0:T(8,128)S(1)}, u32[]{:S(2)}, u32[]{:S(2)}) collective-permute-start(f32[168,128]{1,0:T(8,128)S(1)} %get-tuple-element.28), channel_id=1, source_target_pairs={{0,8},{8,0},{16,24},{24,16},{1,9},{9,1},{17,25},{25,17},{2,10},{10... | collective-permute-start | bytes 258056 | tf_op jit(solution)/shard_map/ppermute | solution.py:58
  17.6 1.6 %collective-permute-start.4 = (f32[168,128]{1,0:T(8,128)S(1)}, f32[168,128]{1,0:T(8,128)S(1)}, u32[]{:S(2)}, u32[]{:S(2)}) collective-permute-start(f32[168,128]{1,0:T(8,128)S(1)} %get-tuple-element.29), channel_id=1, source_target_pairs={{8,16},{16,8},{24,0},{0,24},{9,17},{17,9},{25,1},{1,25},{10,18},{1... | collective-permute-start | bytes 258056 | tf_op jit(solution)/shard_map/ppermute | solution.py:58
  19.2 2.3 %collective-permute-start.7 = (f32[784,128]{1,0:T(8,128)S(1)}, f32[784,128]{1,0:T(8,128)S(1)}, u32[]{:S(2)}, u32[]{:S(2)}) collective-permute-start(f32[784,128]{1,0:T(8,128)S(1)} %relay.2), channel_id=1, source_target_pairs={{0,6},{1,7},{2,0},{3,1},{4,2},{5,3},{6,4},{7,5},{8,14},{9,15},{10,... | collective-permute-start | bytes 1204232 | tf_op jit(solution)/shard_map/ppermute | solution.py:817
  21.5 0.0 collective-permute-done.3.near
  21.5 1.5 %collective-permute-done.4.across = f32[168,128]{1,0:T(8,128)S(1)} collective-permute-done((f32[168,128]{1,0:T(8,128)S(1)}, f32[168,128]{1,0:T(8,128)S(1)}, u32[]{:S(2)}, u32[]{:S(2)}) %collective-permute-start.4) | collective-permute-done | bytes 86048 | tf_op jit(solution)/shard_map/ppermute | solution.py:58
  23.0 4.3 %combine.1.rest_3_.coef_ref = f32[9128,128]{1,0:T(8,128)S(1)} custom-call(f32[4368,128]{1,0:T(8,128)S(1)} %get-tuple-element.27.ring_ref.rest_1_, f32[168,128]{1,0:T(8,128)S(1)} %collective-permute-done.3.near, f32[168,128]{1,0:T(8,128)S(1)} %collective-permute-done.4.across), custom_call_target="tpu_custom_call" | custom-call | tf_op jit(solution)/shard_map/combine/pallas_call | solution.py:483
  27.3 3.0 %collective-permute-done.5.rest_2_ = f32[392,128]{1,0:T(8,128)S(1)} collective-permute-done((f32[392,128]{1,0:T(8,128)S(1)}, f32[392,128]{1,0:T(8,128)S(1)}, u32[]{:S(2)}, u32[]{:S(2)}) %collective-permute-start.5) | collective-permute-done | bytes 200736 | tf_op jit(solution)/shard_map/ppermute | solution.py:817
  30.3 3.5 %scatter_own.1.rest_0_.rest_1_ = f32[7280,128]{1,0:T(8,128)S(1)} custom-call(s32[1,2560]{1,0:T(1,128)S(1)} %constant_dynamic-update-slice_fusion.table_ref, f32[5760,128]{1,0:T(8,128)} %bitcast.24, f32[392,128]{1,0:T(8,128)S(1)} %get-tuple-element.30.rest_0_, f32[1568,128]{1,0:T(8,128)S(1)} %collective-permute-done.2.after.rest_1_.swapped, ...), custom_call_target="tpu_custom_call" | custom-call | tf_op jit(solution)/shard_map/scatter_own/pallas_call | solution.py:313
  33.8 7.8 %collective-permute-start.6 = (f32[392,128]{1,0:T(8,128)S(1)}, f32[392,128]{1,0:T(8,128)S(1)}, u32[]{:S(2)}, u32[]{:S(2)}) collective-permute-start(f32[392,128]{1,0:T(8,128)S(1)} %alone.1), channel_id=1, source_target_pairs={{0,4},{1,5},{2,6},{3,7},{4,0},{5,1},{6,2},{7,3},{8,12},{9,13},{10,... | collective-permute-start | bytes 602120 | tf_op jit(solution)/shard_map/ppermute | solution.py:817
  41.7 0.0 collective-permute-done.8.rest_0_
  41.7 1.8 %scatter_more.2.rest_1_ = f32[7280,128]{1,0:T(8,128)S(1)} custom-call(s32[1,2560]{1,0:T(1,128)S(1)} %constant_dynamic-update-slice_fusion.table_ref, f32[784,128]{1,0:T(8,128)S(1)} %collective-permute-done.8.rest_0_, f32[7280,128]{1,0:T(8,128)S(1)} %scatter_own.1.rest_0_.rest_1_), custom_call_target="tpu_custom_call", output_to_operand_aliasing={{}: (2, {})} | custom-call | tf_op jit(solution)/shard_map/scatter_more/pallas_call | solution.py:370
  43.5 1.7 %scatter_more.3.rest_1_ = f32[7280,128]{1,0:T(8,128)S(1)} custom-call(s32[1,2560]{1,0:T(1,128)S(1)} %constant_dynamic-update-slice_fusion.table_ref, f32[784,128]{1,0:T(8,128)S(1)} %collective-permute-done.7.rest_0_, f32[7280,128]{1,0:T(8,128)S(1)} %scatter_more.2.rest_1_), custom_call_target="tpu_custom_call", output_to_operand_aliasing={{}: (2, {})} | custom-call | tf_op jit(solution)/shard_map/scatter_more/pallas_call | solution.py:370
  45.2 5.3 %collective-permute-done.6.rest_0_ = f32[392,128]{1,0:T(8,128)S(1)} collective-permute-done((f32[392,128]{1,0:T(8,128)S(1)}, f32[392,128]{1,0:T(8,128)S(1)}, u32[]{:S(2)}, u32[]{:S(2)}) %collective-permute-start.6) | collective-permute-done | bytes 200736 | tf_op jit(solution)/shard_map/ppermute | solution.py:817
  50.5 2.1 %scatter_last.1 = (f32[7280,128]{1,0:T(8,128)S(1)}, f32[480,128]{1,0:T(8,128)S(1)}, f32[480,128]{1,0:T(8,128)S(1)}) custom-call(s32[1,2560]{1,0:T(1,128)S(1)} %constant_dynamic-update-slice_fusion.table_ref, f32[392,128]{1,0:T(8,128)S(1)} %collective-permute-done.6.rest_0_, f32[7280,128]{1,0:T(8,128)S(1)} %scatter_more.3.rest_1_), custom_call_target="tpu_custom_call", output_to_operand_aliasing={{0}: (2, {})} | custom-call | tf_op jit(solution)/shard_map/scatter_last/pallas_call | solution.py:370
  52.6 1.4 %collective-permute-start.9 = (f32[480,128]{1,0:T(8,128)S(1)}, f32[480,128]{1,0:T(8,128)S(1)}, u32[]{:S(2)}, u32[]{:S(2)}) collective-permute-start(f32[480,128]{1,0:T(8,128)S(1)} %get-tuple-element.35), channel_id=1, source_target_pairs={{0,1},{1,0},{2,3},{3,2},{4,5},{5,4},{6,7},{7,6},{8,9},{9,8},{10,11... | collective-permute-start | bytes 737288 | tf_op jit(solution)/shard_map/ppermute | solution.py:58
  54.0 2.6 %collective-permute-start.10 = (f32[480,128]{1,0:T(8,128)S(1)}, f32[480,128]{1,0:T(8,128)S(1)}, u32[]{:S(2)}, u32[]{:S(2)}) collective-permute-start(f32[480,128]{1,0:T(8,128)S(1)} %get-tuple-element.36), channel_id=1, source_target_pairs={{1,2},{2,1},{3,4},{4,3},{5,6},{6,5},{9,10},{10,9},{11,12},{12,11},... | collective-permute-start | bytes 737288 | tf_op jit(solution)/shard_map/ppermute | solution.py:58
  56.6 2.7 %early.1.mid_in = f32[6520,128]{1,0:T(8,128)S(1)} custom-call(f32[9128,128]{1,0:T(8,128)S(1)} %combine.1.rest_3_.coef_ref, f32[7280,128]{1,0:T(8,128)S(1)} %get-tuple-element.34.state_in.state), custom_call_target="tpu_custom_call" | custom-call | tf_op jit(solution)/shard_map/early/pallas_call | solution.py:653
  59.3 2.5 %collective-permute-done.10.across = f32[480,128]{1,0:T(8,128)S(1)} collective-permute-done((f32[480,128]{1,0:T(8,128)S(1)}, f32[480,128]{1,0:T(8,128)S(1)}, u32[]{:S(2)}, u32[]{:S(2)}) %collective-permute-start.10) | collective-permute-done | bytes 245792 | tf_op jit(solution)/shard_map/ppermute | solution.py:58
  61.8 0.4 insert.1
  62.2 1.7 %collective-permute-start.11 = (f32[280,128]{1,0:T(8,128)S(1)}, f32[280,128]{1,0:T(8,128)S(1)}, u32[]{:S(2)}, u32[]{:S(2)}) collective-permute-start(f32[280,128]{1,0:T(8,128)S(1)} %get-tuple-element.39), channel_id=1, source_target_pairs={{0,8},{8,0},{16,24},{24,16},{1,9},{9,1},{17,25},{25,17},{2,10},{10... | collective-permute-start | bytes 430088 | tf_op jit(solution)/shard_map/ppermute | solution.py:58
  63.9 5.5 %inner.1 = (f32[6520,128]{1,0:T(8,128)S(1)}, f32[5760,128]{1,0:T(8,128)}) custom-call(f32[9128,128]{1,0:T(8,128)S(1)} %combine.1.rest_3_.coef_ref, f32[7280,128]{1,0:T(8,128)S(1)} %get-tuple-element.37.state.state_in, f32[6520,128]{1,0:T(8,128)S(1)} %early.1.mid_in), custom_call_target="tpu_custom_call", output_to_operand_aliasing={{0}: (2, {})} | custom-call | tf_op jit(solution)/shard_map/inner/pallas_call | solution.py:709
  69.4 1.7 %outer.1 = (f32[7280,128]{1,0:T(8,128)S(1)}, f32[6520,128]{1,0:T(8,128)S(1)}, f32[5760,128]{1,0:T(8,128)}) custom-call(f32[9128,128]{1,0:T(8,128)S(1)} %combine.1.rest_3_.coef_ref, f32[7280,128]{1,0:T(8,128)S(1)} %get-tuple-element.37.state.state_in, ...), custom_call_target="tpu_custom_call", output_to_operand_aliasing={{0}: (1, {}), {1}: (2, {}), {2}: (5, {})} | custom-call | tf_op jit(solution)/shard_map/outer/pallas_call | solution.py:769
  (13 shorter events, 0.1 us)
Async XLA Ops:
  5.1 9.5 %collective-permute-start = (f32[288,128]{1,0:T(8,128)S(1)}, f32[288,128]{1,0:T(8,128)S(1)}, u32[]{:S(2)}, u32[]{:S(2)}) collective-permute-start(f32[288,128]{1,0:T(8,128)S(1)} %get-tuple-element.24), channel_id=1, source_target_pairs={{0,1},{1,0},{2,3},{3,2},{4,5},{5,4},{6,7},{7,6},{8,9},{9,8},{10,11... | collective-permute-start | bytes 442376 | tf_op jit(solution)/shard_map/ppermute | solution.py:58
  5.2 9.5 %collective-permute-start.1 = (f32[288,128]{1,0:T(8,128)S(1)}, f32[288,128]{1,0:T(8,128)S(1)}, u32[]{:S(2)}, u32[]{:S(2)}) collective-permute-start(f32[288,128]{1,0:T(8,128)S(1)} %get-tuple-element.25), channel_id=1, source_target_pairs={{1,2},{2,1},{3,4},{4,3},{5,6},{6,5},{9,10},{10,9},{11,12},{12,11},... | collective-permute-start | bytes 442376 | tf_op jit(solution)/shard_map/ppermute | solution.py:58
  9.5 20.9 %collective-permute-start.5 = (f32[392,128]{1,0:T(8,128)S(1)}, f32[392,128]{1,0:T(8,128)S(1)}, u32[]{:S(2)}, u32[]{:S(2)}) collective-permute-start(f32[392,128]{1,0:T(8,128)S(1)} %get-tuple-element.31), channel_id=1, source_target_pairs={{0,4},{1,5},{2,6},{3,7},{4,0},{5,1},{6,2},{7,3},{8,12},{9,13},{10,... | collective-permute-start | bytes 602120 | tf_op jit(solution)/shard_map/ppermute | solution.py:817
  11.8 2.3 %collective-permute-start.2 = (f32[1568,128]{1,0:T(8,128)S(1)}, f32[1568,128]{1,0:T(8,128)S(1)}, u32[]{:S(2)}, u32[]{:S(2)}) collective-permute-start(f32[1568,128]{1,0:T(8,128)S(1)} %get-tuple-element.26), channel_id=1, source_target_pairs={{0,1},{1,0},{2,3},{3,2},{4,5},{5,4},{6,7},{7,6},{8,9},{9,8},{10,11... | collective-permute-start | bytes 2408456 | tf_op jit(solution)/shard_map/ppermute | solution.py:807
  14.2 27.5 %collective-permute-start.8 = (f32[784,128]{1,0:T(8,128)S(1)}, f32[784,128]{1,0:T(8,128)S(1)}, u32[]{:S(2)}, u32[]{:S(2)}) collective-permute-start(f32[784,128]{1,0:T(8,128)S(1)} %relay.3), channel_id=1, source_target_pairs={{0,2},{1,3},{2,4},{3,5},{4,6},{5,7},{6,0},{7,1},{8,10},{9,11},{10,... | collective-permute-start | bytes 1204232 | tf_op jit(solution)/shard_map/ppermute | solution.py:817
  16.6 4.9 %collective-permute-start.3 = (f32[168,128]{1,0:T(8,128)S(1)}, f32[168,128]{1,0:T(8,128)S(1)}, u32[]{:S(2)}, u32[]{:S(2)}) collective-permute-start(f32[168,128]{1,0:T(8,128)S(1)} %get-tuple-element.28), channel_id=1, source_target_pairs={{0,8},{8,0},{16,24},{24,16},{1,9},{9,1},{17,25},{25,17},{2,10},{10... | collective-permute-start | bytes 258056 | tf_op jit(solution)/shard_map/ppermute | solution.py:58
  17.6 5.4 %collective-permute-start.4 = (f32[168,128]{1,0:T(8,128)S(1)}, f32[168,128]{1,0:T(8,128)S(1)}, u32[]{:S(2)}, u32[]{:S(2)}) collective-permute-start(f32[168,128]{1,0:T(8,128)S(1)} %get-tuple-element.29), channel_id=1, source_target_pairs={{8,16},{16,8},{24,0},{0,24},{9,17},{17,9},{25,1},{1,25},{10,18},{1... | collective-permute-start | bytes 258056 | tf_op jit(solution)/shard_map/ppermute | solution.py:58
  19.2 24.3 %collective-permute-start.7 = (f32[784,128]{1,0:T(8,128)S(1)}, f32[784,128]{1,0:T(8,128)S(1)}, u32[]{:S(2)}, u32[]{:S(2)}) collective-permute-start(f32[784,128]{1,0:T(8,128)S(1)} %relay.2), channel_id=1, source_target_pairs={{0,6},{1,7},{2,0},{3,1},{4,2},{5,3},{6,4},{7,5},{8,14},{9,15},{10,... | collective-permute-start | bytes 1204232 | tf_op jit(solution)/shard_map/ppermute | solution.py:817
  33.8 16.7 %collective-permute-start.6 = (f32[392,128]{1,0:T(8,128)S(1)}, f32[392,128]{1,0:T(8,128)S(1)}, u32[]{:S(2)}, u32[]{:S(2)}) collective-permute-start(f32[392,128]{1,0:T(8,128)S(1)} %alone.1), channel_id=1, source_target_pairs={{0,4},{1,5},{2,6},{3,7},{4,0},{5,1},{6,2},{7,3},{8,12},{9,13},{10,... | collective-permute-start | bytes 602120 | tf_op jit(solution)/shard_map/ppermute | solution.py:817
  52.6 6.7 %collective-permute-start.9 = (f32[480,128]{1,0:T(8,128)S(1)}, f32[480,128]{1,0:T(8,128)S(1)}, u32[]{:S(2)}, u32[]{:S(2)}) collective-permute-start(f32[480,128]{1,0:T(8,128)S(1)} %get-tuple-element.35), channel_id=1, source_target_pairs={{0,1},{1,0},{2,3},{3,2},{4,5},{5,4},{6,7},{7,6},{8,9},{9,8},{10,11... | collective-permute-start | bytes 737288 | tf_op jit(solution)/shard_map/ppermute | solution.py:58
  54.0 7.8 %collective-permute-start.10 = (f32[480,128]{1,0:T(8,128)S(1)}, f32[480,128]{1,0:T(8,128)S(1)}, u32[]{:S(2)}, u32[]{:S(2)}) collective-permute-start(f32[480,128]{1,0:T(8,128)S(1)} %get-tuple-element.36), channel_id=1, source_target_pairs={{1,2},{2,1},{3,4},{4,3},{5,6},{6,5},{9,10},{10,9},{11,12},{12,11},... | collective-permute-start | bytes 737288 | tf_op jit(solution)/shard_map/ppermute | solution.py:58
  62.2 7.2 %collective-permute-start.11 = (f32[280,128]{1,0:T(8,128)S(1)}, f32[280,128]{1,0:T(8,128)S(1)}, u32[]{:S(2)}, u32[]{:S(2)}) collective-permute-start(f32[280,128]{1,0:T(8,128)S(1)} %get-tuple-element.39), channel_id=1, source_target_pairs={{0,8},{8,0},{16,24},{24,16},{1,9},{9,1},{17,25},{25,17},{2,10},{10... | collective-permute-start | bytes 430088 | tf_op jit(solution)/shard_map/ppermute | solution.py:58
  63.9 5.5 %collective-permute-start.12 = (f32[280,128]{1,0:T(8,128)S(1)}, f32[280,128]{1,0:T(8,128)S(1)}, u32[]{:S(2)}, u32[]{:S(2)}) collective-permute-start(f32[280,128]{1,0:T(8,128)S(1)} %get-tuple-element.40), channel_id=1, source_target_pairs={{8,16},{16,8},{24,0},{0,24},{9,17},{17,9},{25,1},{1,25},{10,18},{1... | collective-permute-start | bytes 430088 | tf_op jit(solution)/shard_map/ppermute | solution.py:58
where the time goes:
time: 70.9 us; the launch traced here: 71.1 us
  Pallas kernels  30.1 us (42%)
  starting transfers between devices  25.5 us (36%)
  waiting for transfers between devices  13.9 us (20%)
  between operations  0.82 us (1%)
  other arithmetic  0.75 us (1%)
    ppermute x4, starting transfers between devices, send(): return lax.ppermute(packet, 'lat', [(i, (i + 2 * s) % n) for i in range(n)])  13 us
    ppermute x4, starting transfers between devices, swap_sides(): lax.ppermute(across, axis, across_pairs)  8.4 us
    ppermute x4, waiting for transfers between devices, send(): return lax.ppermute(packet, 'lat', [(i, (i + 2 * s) % n) for i in range(n)])  8.34 us
    pallas_call x3, Pallas kernels, scatter_more(): pl.pallas_call(functools.partial(more_kernel, k, lons, lats, cap, last),...  5.59 us
    pallas_call x1, Pallas kernels, inner(): pl.pallas_call(functools.partial(inner_kernel, lons, lats), out_shape=(V(...  5.49 us
    pallas_call x1, Pallas kernels, pack(): pl.pallas_call(functools.partial(pack_kernel, n, cap, stations), out_shap...  4.47 us
    pallas_call x1, Pallas kernels, combine(): pl.pallas_call(functools.partial(combine_kernel, lons, lats), out_shape=V...  4.32 us
    ppermute x4, starting transfers between devices, swap_sides(): lax.ppermute(near, axis, near_pairs)  4.12 us
  transfers between devices with their start and end apart: 13, of which 5 were waited for; matrix products, arithmetic and copies ran while one was open for 1% of the time, Pallas kernels for 30%

commit v1 on v0

--- a/solution.py
+++ b/solution.py
@@ -69,8 +69,8 @@
     half = n // 2
     own, swap = rest[:2]
     through = rest[2 : half + 1]
-    near, across = rest[half + 1 : half + 3]
-    (dep, band, station, var, edge, buf, pos_v, pos_s, sem) = rest[half + 3 :]
+    across = rest[half + 1]
+    (dep, band, station, var, edge, buf, pos_v, pos_s, sem) = rest[half + 2 :]
     me = lax.axis_index("lat")
     rows, lanes = band.shape
     lat_cells = coef_ref.shape[2]
@@ -157,8 +157,9 @@
 
     def strip(i, carry):
         for f in range(fields):
-            near[pl.ds((f * lons + i) * 2, 2), :] = edge[1 - odd, f, i, pl.ds(6 - 6 * odd, 2), :]
-            across[pl.ds((f * lons + i) * 2, 2), :] = edge[odd, f, i, pl.ds(6 * odd, 2), :]
+            row = (f * lons + i) * 2
+            swap[pl.ds(half * size + row, 2), :] = edge[1 - odd, f, i, pl.ds(6 - 6 * odd, 2), :]
+            across[pl.ds(row, 2), :] = edge[odd, f, i, pl.ds(6 * odd, 2), :]
         return carry
 
     lax.fori_loop(0, lons, strip, 0)
@@ -182,10 +183,10 @@
     fields, lons = coef.shape[:2]
     size, half = cap + HEADER, n // 2
     strip = (fields * lons * 2, LANES)
-    shapes = [(size, LANES), (half * size, LANES)]
+    shapes = [(size, LANES), (half * size + strip[0], LANES)]
     shapes += [
         (size if s == half // 2 else 2 * size, LANES) for s in range(1, half)
-    ] + [strip, strip]
+    ] + [strip]
     hbm = pl.BlockSpec(memory_space=pltpu.HBM)
     vm = pl.BlockSpec(memory_space=V)
     return pl.pallas_call(
@@ -386,10 +387,11 @@
     )
 
 
-def widen_kernel(coef_ref, near_ref, across_ref, after, ring_out, near_lon, across_lon, own, sem):
+def widen_kernel(coef_ref, swapped_ref, across_ref, ring_out, near_lon, across_lon, own, sem):
     fields, lons, lats, _ = coef_ref.shape
     span = lats + 4
     ring = (lons + 4) * span
+    near_from = swapped_ref.shape[0] - fields * lons * 2
     near_row, across_row = near_side(0, lats + 2)
     near_at, across_at = near_side(2 * span, lons * span, "lon")
     run([pltpu.make_async_copy(coef_ref, own, sem)])
@@ -400,7 +402,7 @@
             at = (f * lons + i) * 2
             for r in range(0, lats, 8):
                 ring_out[pl.ds(to + 2 + r, 8), :] = own[f, i, r : r + 8]
-            ring_out[pl.ds(to + near_row, 2), :] = near_ref[pl.ds(at, 2), :]
+            ring_out[pl.ds(to + near_row, 2), :] = swapped_ref[pl.ds(near_from + at, 2), :]
             ring_out[pl.ds(to + across_row, 2), :] = across_ref[pl.ds(at, 2), :]
         return carry
 
@@ -420,7 +422,7 @@
         ring_ref[pl.ds(f * ring + across_at, size), :] = across[pl.ds(f * size, size), :]
 
 
-def widen(coef, near, across, after):
+def widen(coef, swapped, across):
     fields, lons, lats, _ = coef.shape
     span = lats + 4
     vm = pl.BlockSpec(memory_space=V)
@@ -428,12 +430,12 @@
     return pl.pallas_call(
         widen_kernel,
         out_shape=(V((fields * (lons + 4) * span, LANES), jnp.float32), edge, edge),
-        in_specs=[pl.BlockSpec(memory_space=pltpu.HBM), vm, vm, vm],
+        in_specs=[pl.BlockSpec(memory_space=pltpu.HBM), vm, vm],
         out_specs=(vm, vm, vm),
         scratch_shapes=[V(coef.shape, jnp.float32), pltpu.SemaphoreType.DMA],
         compiler_params=params(),
         name="widen",
-    )(in_hbm(coef), in_vmem(near), in_vmem(across), in_vmem(after))
+    )(in_hbm(coef), in_vmem(swapped), in_vmem(across))
 
 
 def combine_kernel(lons, lats, ring_ref, near, across, out_ref, field):
@@ -803,9 +805,9 @@
         departures.reshape(slots, levels),
         coefficients,
     )
-    through, (near, across) = rest[:-2], rest[-2:]
+    through, across = rest[:-1], rest[-1]
     swapped = lax.ppermute(swap, "lat", [(i, i ^ 1) for i in range(n)])
-    near, across = swap_sides(near, across, "lat", False)
+    across = lax.ppermute(across, "lat", pairs_of("lat", False)[1])
     size = cap + HEADER
     order = sorted(range(1, n // 2), key=lambda s: abs(4 * s - n))
     cell = station_cell.reshape(1, stations)
@@ -826,7 +828,7 @@
     adjoint = adjoint_in.reshape(nv * lons * lats, levels)
     ahead = send(order[0], through[order[0] - 1])
     second = send_pairs(order[1:middle], ())
-    ring, near, across = widen(coefficients, near, across, swapped)
+    ring, near, across = widen(coefficients, swapped, across)
     third = send_pairs(order[middle:], (ring,))
     near, across = swap_sides(near, across, "lon", True)
     coef = combine(ring, near, across, lons, lats)

time: 70.9 us -> 69.4 us (0.979); the launches traced: 71.1 us -> 68.8 us
  Pallas kernels: 30.1 us -> 40.1 us
  starting transfers between devices: 25.5 us -> 16.8 us
  waiting for transfers between devices: 13.9 us -> 10.3 us
    pallas_call x3, Pallas kernels: 5.59 us -> 12.2 us  [scatter_more(): pl.pallas_call(functools.partial(more_kernel, k, lons, lats, cap, last),...]
    ppermute x4, starting transfers between devices: 13 us -> 6.43 us  [send(): return lax.ppermute(packet, 'lat', [(i, (i + 2 * s) % n) for i in range(n)])]
    ppermute x0 -> x1, starting transfers between devices: none -> 4.1 us  [body(): across = lax.ppermute(across, 'lat', pairs_of('lat', False)[1])]
    ppermute x4 -> x3, starting transfers between devices: 8.4 us -> 4.78 us  [swap_sides(): lax.ppermute(across, axis, across_pairs)]
    pallas_call x1, Pallas kernels: 3.46 us -> 7.07 us  [scatter_first(): pl.pallas_call(functools.partial(first_kernel, k, lons, lats, cap), out_s...]
    ppermute x4 -> x3, starting transfers between devices: 4.12 us -> 1.4 us  [swap_sides(): lax.ppermute(near, axis, near_pairs)]
    ppermute x4, waiting for transfers between devices: 8.34 us -> 6.22 us  [send(): return lax.ppermute(packet, 'lat', [(i, (i + 2 * s) % n) for i in range(n)])]
    ppermute x1, waiting for transfers between devices: 1.56 us -> 0.01 us  [body(): swapped = lax.ppermute(swap, 'lat', [(i, i ^ 1) for i in range(n)])]
  transfers between devices with their start and end apart: 13 -> 12, of which waited for: 5 -> 4; matrix products, arithmetic and copies ran while one was open for 1% -> 1% of each run, Pallas kernels for 30% -> 44%
where the time goes in v1:
time: 69.4 us; the launch traced here: 68.8 us
  Pallas kernels  40.1 us (58%)
  starting transfers between devices  16.8 us (24%)
  waiting for transfers between devices  10.3 us (15%)
  between operations  0.87 us (1%)
  other arithmetic  0.74 us (1%)
    pallas_call x3, Pallas kernels, scatter_more(): pl.pallas_call(functools.partial(more_kernel, k, lons, lats, cap, last),...  12.2 us
    pallas_call x1, Pallas kernels, scatter_first(): pl.pallas_call(functools.partial(first_kernel, k, lons, lats, cap), out_s...  7.07 us
    ppermute x4, starting transfers between devices, send(): return lax.ppermute(packet, 'lat', [(i, (i + 2 * s) % n) for i in range(n)])  6.43 us
    ppermute x4, waiting for transfers between devices, send(): return lax.ppermute(packet, 'lat', [(i, (i + 2 * s) % n) for i in range(n)])  6.22 us
    pallas_call x1, Pallas kernels, inner(): pl.pallas_call(functools.partial(inner_kernel, lons, lats), out_shape=(V(...  5.49 us
    ppermute x3, starting transfers between devices, swap_sides(): lax.ppermute(across, axis, across_pairs)  4.78 us
    pallas_call x1, Pallas kernels, combine(): pl.pallas_call(functools.partial(combine_kernel, lons, lats), out_shape=V...  4.32 us
    pallas_call x1, Pallas kernels, pack(): pl.pallas_call(functools.partial(pack_kernel, n, cap, stations), out_shap...  4.28 us
  transfers between devices with their start and end apart: 12, of which 4 were waited for; matrix products, arithmetic and copies ran while one was open for 1% of the time, Pallas kernels for 44%

profile of v1, /device:TPU:1, one launch (start us, length us, event | category | flops | bytes accessed | tf_op | source)
XLA Modules:
  0.0 68.8 jit_solution(1275106356604620651)
XLA Ops:
  0.7 4.3 %pack.1 = (f32[392,128]{1,0:T(8,128)S(1)}, f32[1856,128]{1,0:T(8,128)S(1)}, f32[784,128]{1,0:T(8,128)S(1)}, f32[392,128]{1,0:T(8,128)S(1)}, f32[784,128]{1,0:T(8,128)S(1)}, /*index=5*/f32[288,128]{1,0:T(8,128)S(1)}) custom-call(s32[1,1]{1,0:T(1,128)S(6)} %copy.33.count_ref, s32[8,128]{1,0:T(8,128)} %bitcast.26, s32[8,128]{1,0:T(8,128)} %bitcast.27, ...), custom_call_target="tpu_custom_call" | custom-call | tf_op jit(solution)/shard_map/pack/pallas_call | solution.py:192
  4.9 0.1 collective-permute-start
  5.0 4.1 %collective-permute-start.1 = (f32[288,128]{1,0:T(8,128)S(1)}, f32[288,128]{1,0:T(8,128)S(1)}, u32[]{:S(2)}, u32[]{:S(2)}) collective-permute-start(f32[288,128]{1,0:T(8,128)S(1)} %get-tuple-element.24), channel_id=1, source_target_pairs={{1,2},{2,1},{3,4},{4,3},{5,6},{6,5},{9,10},{10,9},{11,12},{12,11},... | collective-permute-start | bytes 442376 | tf_op jit(solution)/shard_map/ppermute | solution.py:810
  9.1 3.1 %collective-permute-start.4 = (f32[392,128]{1,0:T(8,128)S(1)}, f32[392,128]{1,0:T(8,128)S(1)}, u32[]{:S(2)}, u32[]{:S(2)}) collective-permute-start(f32[392,128]{1,0:T(8,128)S(1)} %get-tuple-element.29), channel_id=1, source_target_pairs={{0,4},{1,5},{2,6},{3,7},{4,0},{5,1},{6,2},{7,3},{8,12},{9,13},{10,... | collective-permute-start | bytes 602120 | tf_op jit(solution)/shard_map/ppermute | solution.py:819
  12.2 0.7 %constant_dynamic-update-slice_fusion.4 = (s32[1,2560]{1,0:T(1,128)S(1)}, s32[1,512]{1,0:T(1,128)S(1)}) fusion(s32[1,1,512]{2,1,0:T(1,128)} %param.14), kind=kLoop, calls=%fused_computation.4 | loop fusion | flops 8191 | bytes 6144
  13.0 0.1 collective-permute-start.7
  13.0 0.0 collective-permute-done.1.across_ref
  13.0 1.9 %widen.1 = (f32[4368,128]{1,0:T(8,128)S(1)}, f32[168,128]{1,0:T(8,128)S(1)}, f32[168,128]{1,0:T(8,128)S(1)}) custom-call(f32[3,48,24,128]{3,2,1,0:T(8,128)} %coef_ref.3, f32[1856,128]{1,0:T(8,128)S(1)} %collective-permute-done.swapped_ref.rest_1_.swapped, f32[288,128]{1,0:T(8,128)S(1)} %collective-permute-done.1.across_ref), custom_call_target="tpu_custom_call" | custom-call | tf_op jit(solution)/shard_map/widen/pallas_call | solution.py:430
  15.0 1.1 %collective-permute-start.2 = (f32[168,128]{1,0:T(8,128)S(1)}, f32[168,128]{1,0:T(8,128)S(1)}, u32[]{:S(2)}, u32[]{:S(2)}) collective-permute-start(f32[168,128]{1,0:T(8,128)S(1)} %get-tuple-element.26), channel_id=1, source_target_pairs={{0,8},{8,0},{16,24},{24,16},{1,9},{9,1},{17,25},{25,17},{2,10},{10... | collective-permute-start | bytes 258056 | tf_op jit(solution)/shard_map/ppermute | solution.py:58
  16.0 1.3 %collective-permute-start.3 = (f32[168,128]{1,0:T(8,128)S(1)}, f32[168,128]{1,0:T(8,128)S(1)}, u32[]{:S(2)}, u32[]{:S(2)}) collective-permute-start(f32[168,128]{1,0:T(8,128)S(1)} %get-tuple-element.27), channel_id=1, source_target_pairs={{8,16},{16,8},{24,0},{0,24},{9,17},{17,9},{25,1},{1,25},{10,18},{1... | collective-permute-start | bytes 258056 | tf_op jit(solution)/shard_map/ppermute | solution.py:58
  17.3 3.2 %collective-permute-start.6 = (f32[784,128]{1,0:T(8,128)S(1)}, f32[784,128]{1,0:T(8,128)S(1)}, u32[]{:S(2)}, u32[]{:S(2)}) collective-permute-start(f32[784,128]{1,0:T(8,128)S(1)} %relay.2), channel_id=1, source_target_pairs={{0,6},{1,7},{2,0},{3,1},{4,2},{5,3},{6,4},{7,5},{8,14},{9,15},{10,... | collective-permute-start | bytes 1204232 | tf_op jit(solution)/shard_map/ppermute | solution.py:819
  20.6 0.0 collective-permute-done.2.near
  20.6 0.9 %collective-permute-done.3.across = f32[168,128]{1,0:T(8,128)S(1)} collective-permute-done((f32[168,128]{1,0:T(8,128)S(1)}, f32[168,128]{1,0:T(8,128)S(1)}, u32[]{:S(2)}, u32[]{:S(2)}) %collective-permute-start.3) | collective-permute-done | bytes 86048 | tf_op jit(solution)/shard_map/ppermute | solution.py:58
  21.5 4.3 %combine.1.rest_3_.coef_ref = f32[9128,128]{1,0:T(8,128)S(1)} custom-call(f32[4368,128]{1,0:T(8,128)S(1)} %get-tuple-element.25.ring_ref.rest_1_, f32[168,128]{1,0:T(8,128)S(1)} %collective-permute-done.2.near, f32[168,128]{1,0:T(8,128)S(1)} %collective-permute-done.3.across), custom_call_target="tpu_custom_call" | custom-call | tf_op jit(solution)/shard_map/combine/pallas_call | solution.py:485
  25.8 4.9 %collective-permute-done.4.rest_2_ = f32[392,128]{1,0:T(8,128)S(1)} collective-permute-done((f32[392,128]{1,0:T(8,128)S(1)}, f32[392,128]{1,0:T(8,128)S(1)}, u32[]{:S(2)}, u32[]{:S(2)}) %collective-permute-start.4) | collective-permute-done | bytes 200736 | tf_op jit(solution)/shard_map/ppermute | solution.py:819
  30.7 7.1 %scatter_own.1.rest_0_.rest_1_ = f32[7280,128]{1,0:T(8,128)S(1)} custom-call(s32[1,2560]{1,0:T(1,128)S(1)} %constant_dynamic-update-slice_fusion.table_ref, f32[5760,128]{1,0:T(8,128)} %bitcast.24, f32[392,128]{1,0:T(8,128)S(1)} %get-tuple-element.28.rest_0_, f32[1856,128]{1,0:T(8,128)S(1)} %collective-permute-done.swapped_ref.rest_1_.swapped, ...), custom_call_target="tpu_custom_call" | custom-call | tf_op jit(solution)/shard_map/scatter_own/pallas_call | solution.py:314
  37.8 0.1 collective-permute-start.5
  37.9 4.7 %scatter_more.2.rest_1_ = f32[7280,128]{1,0:T(8,128)S(1)} custom-call(s32[1,2560]{1,0:T(1,128)S(1)} %constant_dynamic-update-slice_fusion.table_ref, f32[784,128]{1,0:T(8,128)S(1)} %collective-permute-done.7.rest_0_, f32[7280,128]{1,0:T(8,128)S(1)} %scatter_own.1.rest_0_.rest_1_), custom_call_target="tpu_custom_call", output_to_operand_aliasing={{}: (2, {})} | custom-call | tf_op jit(solution)/shard_map/scatter_more/pallas_call | solution.py:371
  42.7 0.0 collective-permute-done.6.rest_0_
  42.7 3.9 %scatter_more.3.rest_1_ = f32[7280,128]{1,0:T(8,128)S(1)} custom-call(s32[1,2560]{1,0:T(1,128)S(1)} %constant_dynamic-update-slice_fusion.table_ref, f32[784,128]{1,0:T(8,128)S(1)} %collective-permute-done.6.rest_0_, f32[7280,128]{1,0:T(8,128)S(1)} %scatter_more.2.rest_1_), custom_call_target="tpu_custom_call", output_to_operand_aliasing={{}: (2, {})} | custom-call | tf_op jit(solution)/shard_map/scatter_more/pallas_call | solution.py:371
  46.6 1.3 %collective-permute-done.5.rest_0_ = f32[392,128]{1,0:T(8,128)S(1)} collective-permute-done((f32[392,128]{1,0:T(8,128)S(1)}, f32[392,128]{1,0:T(8,128)S(1)}, u32[]{:S(2)}, u32[]{:S(2)}) %collective-permute-start.5) | collective-permute-done | bytes 200736 | tf_op jit(solution)/shard_map/ppermute | solution.py:819
  47.9 3.5 %scatter_last.1 = (f32[7280,128]{1,0:T(8,128)S(1)}, f32[480,128]{1,0:T(8,128)S(1)}, f32[480,128]{1,0:T(8,128)S(1)}) custom-call(s32[1,2560]{1,0:T(1,128)S(1)} %constant_dynamic-update-slice_fusion.table_ref, f32[392,128]{1,0:T(8,128)S(1)} %collective-permute-done.5.rest_0_, f32[7280,128]{1,0:T(8,128)S(1)} %scatter_more.3.rest_1_), custom_call_target="tpu_custom_call", output_to_operand_aliasing={{0}: (2, {})} | custom-call | tf_op jit(solution)/shard_map/scatter_last/pallas_call | solution.py:371
  51.4 0.1 collective-permute-start.8
  51.5 1.9 %collective-permute-start.9 = (f32[480,128]{1,0:T(8,128)S(1)}, f32[480,128]{1,0:T(8,128)S(1)}, u32[]{:S(2)}, u32[]{:S(2)}) collective-permute-start(f32[480,128]{1,0:T(8,128)S(1)} %get-tuple-element.34), channel_id=1, source_target_pairs={{1,2},{2,1},{3,4},{4,3},{5,6},{6,5},{9,10},{10,9},{11,12},{12,11},... | collective-permute-start | bytes 737288 | tf_op jit(solution)/shard_map/ppermute | solution.py:58
  53.4 2.7 %early.1.mid_in = f32[6520,128]{1,0:T(8,128)S(1)} custom-call(f32[9128,128]{1,0:T(8,128)S(1)} %combine.1.rest_3_.coef_ref, f32[7280,128]{1,0:T(8,128)S(1)} %get-tuple-element.32.state_in.state), custom_call_target="tpu_custom_call" | custom-call | tf_op jit(solution)/shard_map/early/pallas_call | solution.py:655
  56.2 0.0 collective-permute-done.8.near
  56.2 3.2 %collective-permute-done.9.across = f32[480,128]{1,0:T(8,128)S(1)} collective-permute-done((f32[480,128]{1,0:T(8,128)S(1)}, f32[480,128]{1,0:T(8,128)S(1)}, u32[]{:S(2)}, u32[]{:S(2)}) %collective-permute-start.9) | collective-permute-done | bytes 245792 | tf_op jit(solution)/shard_map/ppermute | solution.py:58
  59.3 0.4 insert.1
  59.7 0.3 collective-permute-start.10
  60.0 1.6 %collective-permute-start.11 = (f32[280,128]{1,0:T(8,128)S(1)}, f32[280,128]{1,0:T(8,128)S(1)}, u32[]{:S(2)}, u32[]{:S(2)}) collective-permute-start(f32[280,128]{1,0:T(8,128)S(1)} %get-tuple-element.38), channel_id=1, source_target_pairs={{8,16},{16,8},{24,0},{0,24},{9,17},{17,9},{25,1},{1,25},{10,18},{1... | collective-permute-start | bytes 430088 | tf_op jit(solution)/shard_map/ppermute | solution.py:58
  61.6 5.5 %inner.1 = (f32[6520,128]{1,0:T(8,128)S(1)}, f32[5760,128]{1,0:T(8,128)}) custom-call(f32[9128,128]{1,0:T(8,128)S(1)} %combine.1.rest_3_.coef_ref, f32[7280,128]{1,0:T(8,128)S(1)} %get-tuple-element.35.state.state_in, f32[6520,128]{1,0:T(8,128)S(1)} %early.1.mid_in), custom_call_target="tpu_custom_call", output_to_operand_aliasing={{0}: (2, {})} | custom-call | tf_op jit(solution)/shard_map/inner/pallas_call | solution.py:711
  67.1 1.7 %outer.1 = (f32[7280,128]{1,0:T(8,128)S(1)}, f32[6520,128]{1,0:T(8,128)S(1)}, f32[5760,128]{1,0:T(8,128)}) custom-call(f32[9128,128]{1,0:T(8,128)S(1)} %combine.1.rest_3_.coef_ref, f32[7280,128]{1,0:T(8,128)S(1)} %get-tuple-element.35.state.state_in, ...), custom_call_target="tpu_custom_call", output_to_operand_aliasing={{0}: (1, {}), {1}: (2, {}), {2}: (5, {})} | custom-call | tf_op jit(solution)/shard_map/outer/pallas_call | solution.py:771
  (11 shorter events, 0.1 us)
Async XLA Ops:
  4.9 8.0 %collective-permute-start = (f32[1856,128]{1,0:T(8,128)S(1)}, f32[1856,128]{1,0:T(8,128)S(1)}, u32[]{:S(2)}, u32[]{:S(2)}) collective-permute-start(f32[1856,128]{1,0:T(8,128)S(1)} %get-tuple-element.23), channel_id=1, source_target_pairs={{0,1},{1,0},{2,3},{3,2},{4,5},{5,4},{6,7},{7,6},{8,9},{9,8},{10,11... | collective-permute-start | bytes 2850824 | tf_op jit(solution)/shard_map/ppermute | solution.py:809
  5.0 8.0 %collective-permute-start.1 = (f32[288,128]{1,0:T(8,128)S(1)}, f32[288,128]{1,0:T(8,128)S(1)}, u32[]{:S(2)}, u32[]{:S(2)}) collective-permute-start(f32[288,128]{1,0:T(8,128)S(1)} %get-tuple-element.24), channel_id=1, source_target_pairs={{1,2},{2,1},{3,4},{4,3},{5,6},{6,5},{9,10},{10,9},{11,12},{12,11},... | collective-permute-start | bytes 442376 | tf_op jit(solution)/shard_map/ppermute | solution.py:810
  9.1 21.6 %collective-permute-start.4 = (f32[392,128]{1,0:T(8,128)S(1)}, f32[392,128]{1,0:T(8,128)S(1)}, u32[]{:S(2)}, u32[]{:S(2)}) collective-permute-start(f32[392,128]{1,0:T(8,128)S(1)} %get-tuple-element.29), channel_id=1, source_target_pairs={{0,4},{1,5},{2,6},{3,7},{4,0},{5,1},{6,2},{7,3},{8,12},{9,13},{10,... | collective-permute-start | bytes 602120 | tf_op jit(solution)/shard_map/ppermute | solution.py:819
  13.0 24.9 %collective-permute-start.7 = (f32[784,128]{1,0:T(8,128)S(1)}, f32[784,128]{1,0:T(8,128)S(1)}, u32[]{:S(2)}, u32[]{:S(2)}) collective-permute-start(f32[784,128]{1,0:T(8,128)S(1)} %relay.3), channel_id=1, source_target_pairs={{0,2},{1,3},{2,4},{3,5},{4,6},{5,7},{6,0},{7,1},{8,10},{9,11},{10,... | collective-permute-start | bytes 1204232 | tf_op jit(solution)/shard_map/ppermute | solution.py:819
  15.0 5.6 %collective-permute-start.2 = (f32[168,128]{1,0:T(8,128)S(1)}, f32[168,128]{1,0:T(8,128)S(1)}, u32[]{:S(2)}, u32[]{:S(2)}) collective-permute-start(f32[168,128]{1,0:T(8,128)S(1)} %get-tuple-element.26), channel_id=1, source_target_pairs={{0,8},{8,0},{16,24},{24,16},{1,9},{9,1},{17,25},{25,17},{2,10},{10... | collective-permute-start | bytes 258056 | tf_op jit(solution)/shard_map/ppermute | solution.py:58
  16.0 5.4 %collective-permute-start.3 = (f32[168,128]{1,0:T(8,128)S(1)}, f32[168,128]{1,0:T(8,128)S(1)}, u32[]{:S(2)}, u32[]{:S(2)}) collective-permute-start(f32[168,128]{1,0:T(8,128)S(1)} %get-tuple-element.27), channel_id=1, source_target_pairs={{8,16},{16,8},{24,0},{0,24},{9,17},{17,9},{25,1},{1,25},{10,18},{1... | collective-permute-start | bytes 258056 | tf_op jit(solution)/shard_map/ppermute | solution.py:58
  17.3 25.3 %collective-permute-start.6 = (f32[784,128]{1,0:T(8,128)S(1)}, f32[784,128]{1,0:T(8,128)S(1)}, u32[]{:S(2)}, u32[]{:S(2)}) collective-permute-start(f32[784,128]{1,0:T(8,128)S(1)} %relay.2), channel_id=1, source_target_pairs={{0,6},{1,7},{2,0},{3,1},{4,2},{5,3},{6,4},{7,5},{8,14},{9,15},{10,... | collective-permute-start | bytes 1204232 | tf_op jit(solution)/shard_map/ppermute | solution.py:819
  37.8 10.1 %collective-permute-start.5 = (f32[392,128]{1,0:T(8,128)S(1)}, f32[392,128]{1,0:T(8,128)S(1)}, u32[]{:S(2)}, u32[]{:S(2)}) collective-permute-start(f32[392,128]{1,0:T(8,128)S(1)} %alone.1), channel_id=1, source_target_pairs={{0,4},{1,5},{2,6},{3,7},{4,0},{5,1},{6,2},{7,3},{8,12},{9,13},{10,... | collective-permute-start | bytes 602120 | tf_op jit(solution)/shard_map/ppermute | solution.py:819
  51.4 4.7 %collective-permute-start.8 = (f32[480,128]{1,0:T(8,128)S(1)}, f32[480,128]{1,0:T(8,128)S(1)}, u32[]{:S(2)}, u32[]{:S(2)}) collective-permute-start(f32[480,128]{1,0:T(8,128)S(1)} %get-tuple-element.33), channel_id=1, source_target_pairs={{0,1},{1,0},{2,3},{3,2},{4,5},{5,4},{6,7},{7,6},{8,9},{9,8},{10,11... | collective-permute-start | bytes 737288 | tf_op jit(solution)/shard_map/ppermute | solution.py:58
  51.5 7.8 %collective-permute-start.9 = (f32[480,128]{1,0:T(8,128)S(1)}, f32[480,128]{1,0:T(8,128)S(1)}, u32[]{:S(2)}, u32[]{:S(2)}) collective-permute-start(f32[480,128]{1,0:T(8,128)S(1)} %get-tuple-element.34), channel_id=1, source_target_pairs={{1,2},{2,1},{3,4},{4,3},{5,6},{6,5},{9,10},{10,9},{11,12},{12,11},... | collective-permute-start | bytes 737288 | tf_op jit(solution)/shard_map/ppermute | solution.py:58
  59.7 7.4 %collective-permute-start.10 = (f32[280,128]{1,0:T(8,128)S(1)}, f32[280,128]{1,0:T(8,128)S(1)}, u32[]{:S(2)}, u32[]{:S(2)}) collective-permute-start(f32[280,128]{1,0:T(8,128)S(1)} %get-tuple-element.37), channel_id=1, source_target_pairs={{0,8},{8,0},{16,24},{24,16},{1,9},{9,1},{17,25},{25,17},{2,10},{10... | collective-permute-start | bytes 430088 | tf_op jit(solution)/shard_map/ppermute | solution.py:58
  60.0 7.1 %collective-permute-start.11 = (f32[280,128]{1,0:T(8,128)S(1)}, f32[280,128]{1,0:T(8,128)S(1)}, u32[]{:S(2)}, u32[]{:S(2)}) collective-permute-start(f32[280,128]{1,0:T(8,128)S(1)} %get-tuple-element.38), channel_id=1, source_target_pairs={{8,16},{16,8},{24,0},{0,24},{9,17},{17,9},{25,1},{1,25},{10,18},{1... | collective-permute-start | bytes 430088 | tf_op jit(solution)/shard_map/ppermute | solution.py:58
